TPU v7x, 256 devices: a whole 4x4x8 slice. The times are simulated.
256 devices in a mesh: sub: 32 (over y, x, core), grp: 8 (over z).
Axes of the slice: x: 4, y: 4, z: 8, core: 2. Of those that a mesh axis runs over, the one named last changes fastest.
Arguments:
- residual: bfloat16 [8, 32, 1024, 512], P('grp', 'sub'), may hold values from -6 to 6
- face_order: int32 [8, 32, 1024], P('grp', 'sub'), may hold values from 0 to 1023, each once within a row
- stiffness: float32 [8, 32], replicated, may hold values from 1 to 100
- schur: bfloat16 [8, 32, 1024, 1024], P('grp', 'sub')
- local_inverse: bfloat16 [8, 32, 1024, 1024], P('grp', 'sub')
- coarse_basis: bfloat16 [8, 32, 1024, 128], P('grp', 'sub'), may hold values from -0.1875 to 0.1875
- coarse_map: int32 [8, 32, 128], P('grp', 'sub'), may hold values from 0 to 511, as said below
- level2_inverse: float32 [8, 512, 512], P('grp')
- level2_basis: float32 [8, 512, 128], P('grp'), may hold values from -0.25 to 0.25
- level2_map: int32 [8, 128], P('grp'), may hold values from 0 to 511, as said below
- level3_inverse: float32 [512, 512], replicated
Outputs:
- solution: bfloat16 [8, 32, 1024, 512], P('grp', 'sub')
- image: bfloat16 [8, 32, 1024, 512], P('grp', 'sub')
Inputs may be any that keep to these rules, and one draw needn't show every extreme that they name: `face_order`: each subdomain's row holds every number of 0 to 1023 once. `coarse_map`: within one subdomain the 128 entries are distinct, and each of a group's 512 level-2 coarse values is named by some subdomain of the group. `level2_map`: within one group the 128 entries are distinct, and each level-3 coarse value is named by some group.
All inputs are finite; a program needn't handle non-finite values.
Results may differ from a plain program's by a relative error of at most 0.0062.
Values may be sent and summed in bfloat16 or wider, within the bound.
A program may use at most 64 MiB of HBM per device.

v0:
```python
import jax
import jax.numpy as jnp
from jax import lax
from jax.sharding import PartitionSpec as P

highest = lax.Precision.HIGHEST


def extended(cells, sides, width):
    for axis, dim in sides:
        count = lax.axis_size(axis)
        ends = count - 1
        head = lax.slice_in_dim(cells, 0, width, axis=dim)
        tail = lax.slice_in_dim(cells, cells.shape[dim] - width, cells.shape[dim], axis=dim)
        cells = jnp.concatenate(
            [
                lax.ppermute(tail, axis, [(i, (i + 1) % count) for i in range(ends)]),
                cells,
                lax.ppermute(head, axis, [((i + 1) % count, i) for i in range(ends)]),
            ],
            axis=dim,
        )
    return cells


def face_weights(stiffness, group_index, member_index):
    group_count, member_count = stiffness.shape
    itself = stiffness[group_index, member_index]

    def share_of(other_group, other_member, present):
        neighbour = stiffness[
            jnp.clip(other_group, 0, group_count - 1), jnp.clip(other_member, 0, member_count - 1)
        ]
        return jnp.where(present, itself / (itself + neighbour), jnp.float32(1.0))

    return jnp.stack(
        [
            share_of(group_index, member_index - 1, member_index > 0),
            share_of(group_index, member_index + 1, member_index < member_count - 1),
            share_of(group_index - 1, member_index, group_index > 0),
            share_of(group_index + 1, member_index, group_index < group_count - 1),
        ]
    )


def shards(
    residual,
    face_order,
    stiffness,
    schur,
    local_inverse,
    coarse_basis,
    coarse_map,
    level2_inverse,
    level2_basis,
    level2_map,
    level3_inverse,
):
    resid_block = residual[0, 0]
    interface_size, columns = resid_block.shape
    face_size = interface_size // 4
    ordering = face_order[0, 0]
    inverse = jnp.argsort(ordering)
    group_index = lax.axis_index("grp")
    member_index = lax.axis_index("sub")
    weights = face_weights(stiffness, group_index, member_index)
    face_of = inverse // face_size
    dof_weight = jnp.sum(
        jnp.where(face_of[:, None] == jnp.arange(4)[None, :], weights[None, :], jnp.float32(0.0)),
        axis=1,
    )
    weighted = (dof_weight[:, None] * resid_block.astype(jnp.float32)).astype(jnp.bfloat16)
    contract_rows = (((0,), (0,)), ((), ()))
    coarse_base = coarse_basis[0, 0]
    coarse_res = lax.dot_general(
        coarse_base, weighted, contract_rows, preferred_element_type=jnp.float32
    )
    level2_size = level2_inverse.shape[1]
    local_map = coarse_map[0, 0]
    selector = (local_map[None, :] == jnp.arange(level2_size)[:, None]).astype(jnp.float32)
    contribution = jnp.dot(selector, coarse_res, precision=highest)
    group_base = level2_basis[0]
    group_map = level2_map[0]
    level3_size = level3_inverse.shape[0]
    selector_three = (group_map[None, :] == jnp.arange(level3_size)[:, None]).astype(jnp.float32)
    local_part = jnp.dot(local_inverse[0, 0], weighted, preferred_element_type=jnp.float32)
    group_inverse = level2_inverse[0]
    level2_res = lax.psum(contribution, "sub")
    group_terms = lax.dot_general(group_base, level2_res, contract_rows, precision=highest)
    level3_res = lax.psum(jnp.dot(selector_three, group_terms, precision=highest), "grp")
    level2_local = jnp.dot(group_inverse, level2_res, precision=highest)
    level3_sol = jnp.dot(level3_inverse, level3_res, precision=highest)
    level2_sol = level2_local + jnp.dot(group_base, level3_sol[group_map], precision=highest)
    coarse_part = jnp.dot(coarse_base.astype(jnp.float32), level2_sol[local_map], precision=highest)
    sendable = (dof_weight[:, None] * (local_part + coarse_part)).astype(jnp.bfloat16)
    face_blocks = sendable[ordering].reshape(4, face_size, columns)
    sub_padded = extended(face_blocks[0:2], (("sub", 0),), 1)
    grp_padded = extended(face_blocks[2:4], (("grp", 0),), 1)
    received = jnp.stack([sub_padded[0], sub_padded[3], grp_padded[0], grp_padded[3]])
    summed = (face_blocks.astype(jnp.float32) + received.astype(jnp.float32)).astype(jnp.bfloat16)
    solution = summed.reshape(interface_size, columns)[inverse]
    image = jnp.dot(schur[0, 0], solution, preferred_element_type=jnp.float32).astype(jnp.bfloat16)
    return (solution[None, None], image[None, None])


def solution(mesh):
    placed = (
        P("grp", "sub", None, None),
        P("grp", "sub", None),
        P(),
        P("grp", "sub", None, None),
        P("grp", "sub", None, None),
        P("grp", "sub", None, None),
        P("grp", "sub", None),
        P("grp", None, None),
        P("grp", None, None),
        P("grp", None),
        P(),
    )
    return jax.shard_map(
        shards,
        mesh=mesh,
        in_specs=placed,
        out_specs=(P("grp", "sub", None, None), P("grp", "sub", None, None)),
        check_vma=False,
    )
```

profile of v0, /device:TPU:8, one launch (start us, length us, event | category | flops | bytes accessed | tf_op | source)
XLA Modules:
  0.0 290.3 jit_solution(15084661443975097650)
XLA Ops:
  7.2 0.0 copy-start
  7.2 0.0 all-reduce.3.cloned.1.call-start
  7.2 1.6 fusion.33
  16.3 5.1 %sort.17 = (s32[1024]{0:T(1024)}, s32[1024]{0:T(1024)S(1)}) sort(s32[1024]{0:T(1024)} %bitcast.82, s32[1024]{0:T(1024)S(1)} %iota.13), dimensions={0}, to_apply=%region_0.0 | sort | flops 10240 | bytes 16384 | tf_op jit(solution)/shard_map/jit(argsort)/sort | solution.py:63
  21.4 0.0 copy-start.6
  21.4 0.1 pad_maximum_fusion.1
  21.5 0.0 copy-start.4
  21.5 0.1 select_reduce_fusion
  21.6 1.9 fusion.15
  23.6 2.2 fusion.24
  25.8 0.0 all-reduce.3.cloned.1.call-update
  25.8 0.0 copy-start.7
  25.8 0.0 copy-start.5
  25.8 0.0 all-reduce.5.cloned.1.call-start
  25.9 0.0 copy-done.6
  25.9 117.2 %all-reduce.3.cloned.1.call-done = f32[512,512]{1,0:T(8,128)} async-done(((f32[512,512]{1,0:T(8,128)}), f32[512,512]{1,0:T(8,128)}) %all-reduce.3.cloned.1.call-update) | async-done | bytes 1048592 | tf_op jit(solution)/shard_map/psum | solution.py:88
  143.2 0.0 copy-done.4
  143.2 3.0 %fusion.20 = f32[512,128]{1,0:T(8,128)S(1)} fusion(f32[512,512]{1,0:T(8,128)} %all-reduce.3.cloned.1.call-done, f32[1,512,128]{2,1,0:T(8,128)S(1)} %copy-done.4), kind=kOutput, calls=%fused_computation.28 | convolution fusion | flops 402653184 | bytes 1572864 | tf_op jit(solution)/shard_map/dot_general | solution.py:89
  146.2 1.6 fusion.25
  147.8 0.0 all-reduce.5.cloned.1.call-update
  147.8 0.0 copy-done.7
  147.8 0.0 copy-done.5
  147.9 0.0 copy-done
  147.9 0.0 copy-start.3
  147.9 4.2 %fusion.3 = f32[512,1024]{1,0:T(8,128)} fusion(bf16[1,1,1024,1024]{3,2,1,0:T(8,128)(2,1)S(1)} %copy-done, bf16[1,1,1024,512]{3,2,1,0:T(8,128)(2,1)} %param.11, f32[1024]{0:T(1024)S(1)} %select_reduce_fusion), kind=kOutput, calls=%fused_computation.8 | convolution fusion | flops 1075314688 | bytes 5246976 | tf_op jit(solution)/shard_map/dot_general | solution.py:86
  152.1 72.2 %all-reduce.5.cloned.1.call-done = f32[512,512]{1,0:T(8,128)} async-done(((f32[512,512]{1,0:T(8,128)}), f32[512,512]{1,0:T(8,128)}) %all-reduce.5.cloned.1.call-update) | async-done | bytes 1048592 | tf_op jit(solution)/shard_map/psum | solution.py:90
  224.3 0.0 copy-done.3
  224.3 5.7 %convolution_bitcast_fusion = f32[512,512]{0,1:T(8,128)} fusion(f32[512,512]{1,0:T(8,128)} %all-reduce.5.cloned.1.call-done, f32[512,512]{1,0:T(8,128)S(1)} %copy-done.3), kind=kOutput, calls=%fused_computation.15 | convolution fusion | flops 1610612736 | bytes 3145728 | tf_op jit(solution)/shard_map/dot_general | solution.py:92
  230.0 1.6 copy.17
  231.5 0.8 gather_fusion
  232.3 0.0 copy-start.2
  232.3 2.1 fusion.18
  234.4 0.0 copy-done.2
  234.4 5.7 %fusion.12 = f32[512,512]{0,1:T(8,128)} fusion(f32[512,512]{1,0:T(8,128)S(1)} %fusion.18, f32[512,512]{1,0:T(8,128)S(1)} %copy-done.2, f32[1,512,512]{2,1,0:T(8,128)} %param.18), kind=kOutput, calls=%fused_computation.17 | convolution fusion | flops 1610874880 | bytes 4194304 | tf_op jit(solution)/shard_map/dot_general | solution.py:91
  240.1 1.7 copy.18
  241.8 0.8 gather_fusion.1
  242.5 3.7 %fusion.11 = bf16[1024,512]{0,1:T(8,128)(2,1)} fusion(f32[512,1024]{1,0:T(8,128)} %fusion.3, f32[128,512]{1,0:T(8,128)S(1)} %gather_fusion.1, f32[1024]{0:T(1024)S(1)} %select_reduce_fusion, bf16[1,1,1024,128]{3,2,1,0:T(8,128)(2,1)} %param.16), kind=kOutput, calls=%fused_computation.14 | convolution fusion | flops 806879232 | bytes 3674112 | tf_op jit(solution)/shard_map/dot_general | solution.py:94
  246.3 1.5 copy.19
  247.8 5.1 %gather_fusion.2 = bf16[1024,512]{1,0:T(8,128)(2,1)} fusion(bf16[1024,512]{1,0:T(8,128)(2,1)S(1)} %copy.19, s32[1024]{0:T(1024)S(1)} %broadcast_clamp_fusion), kind=kCustom, calls=%fused_computation.2 | custom fusion | bytes 2101248 | tf_op jit(solution)/shard_map/gather | solution.py:96
  252.9 0.0 copy-start.1
  252.9 1.3 slice_bitcast_fusion.3
  254.2 1.9 collective-permute-start
  256.2 5.8 %collective-permute-start.1 = (bf16[1,256,512]{2,1,0:T(8,128)(2,1)S(1)}, bf16[1,256,512]{2,1,0:T(8,128)(2,1)S(1)}, u32[]{:S(2)}, u32[]{:S(2)}) collective-permute-start(bf16[1,256,512]{2,1,0:T(8,128)(2,1)S(1)} %get-tuple-element.12), channel_id=1, source_target_pairs={{8,0},{16,8},{24,16},{32,24},{40,32},{48,40},{56,48},{64,56},{72,6... | collective-permute-start | bytes 786440 | tf_op jit(solution)/shard_map/ppermute | solution.py:19
  261.9 3.1 %collective-permute-start.2 = (bf16[1,256,512]{2,1,0:T(8,128)(2,1)S(1)}, bf16[1,256,512]{2,1,0:T(8,128)(2,1)S(1)}, u32[]{:S(2)}, u32[]{:S(2)}) collective-permute-start(bf16[1,256,512]{2,1,0:T(8,128)(2,1)S(1)} %get-tuple-element.11), channel_id=1, source_target_pairs={{0,1},{1,2},{2,3},{3,4},{4,5},{5,6},{6,7},{8,9},{9,10},{10,11},{11... | collective-permute-start | bytes 786440 | tf_op jit(solution)/shard_map/ppermute | solution.py:17
  265.1 1.3 collective-permute-start.3
  266.4 0.0 collective-permute-done
  266.4 0.0 collective-permute-done.1
  266.4 2.5 collective-permute-done.2
  268.9 4.4 %collective-permute-done.3 = bf16[1,256,512]{2,1,0:T(8,128)(2,1)S(1)} collective-permute-done((bf16[1,256,512]{2,1,0:T(8,128)(2,1)S(1)}, bf16[1,256,512]{2,1,0:T(8,128)(2,1)S(1)}, u32[]{:S(2)}, u32[]{:S(2)}) %collective-permute-start.3) | collective-permute-done | bytes 262176 | tf_op jit(solution)/shard_map/ppermute | solution.py:19
  273.3 0.1 pad_maximum_fusion
  273.5 0.0 copy-done.1
  273.5 0.4 fusion
  273.9 5.1 %gather_fusion.3 = bf16[1024,512]{1,0:T(8,128)(2,1)} fusion(bf16[1024,512]{1,0:T(8,128)(2,1)S(1)} %fusion, s32[1024]{0:T(1024)S(1)} %get-tuple-element.14), kind=kCustom, calls=%fused_computation.3 | custom fusion | bytes 2101248 | tf_op jit(solution)/shard_map/gather | solution.py:101
  278.9 3.2 %fusion.8 = bf16[1,1,1024,512]{2,3,1,0:T(8,128)(2,1)S(1)} fusion(bf16[1024,512]{1,0:T(8,128)(2,1)} %gather_fusion.3, bf16[1,1,1024,1024]{3,2,1,0:T(8,128)(2,1)} %param.14), kind=kOutput, calls=%fused_computation.13 | convolution fusion | flops 1074266112 | bytes 4194304 | tf_op jit(solution)/shard_map/dot_general | solution.py:102
  282.2 1.3 copy.20
  (8 shorter events, 0.0 us)
Async XLA Ops:
  7.2 140.7 %copy-start = (bf16[1,1,1024,1024]{3,2,1,0:T(8,128)(2,1)S(1)}, bf16[1,1,1024,1024]{3,2,1,0:T(8,128)(2,1)}, u32[]{:S(2)}) copy-start(bf16[1,1,1024,1024]{3,2,1,0:T(8,128)(2,1)} %param.15) | copy-start | bytes 6291460
  7.2 136.0 %all-reduce.3.cloned.1.call-start = ((), (), s32[]{:S(2)}) async-start(), calls=%async_computation | async-start | bytes 2097152 | tf_op jit(solution)/shard_map/psum | solution.py:88
  21.4 4.5 %copy-start.6 = (s32[1,128]{1,0:T(1,128)S(1)}, s32[1,128]{1,0:T(1,128)}, u32[]{:S(2)}) copy-start(s32[1,128]{1,0:T(1,128)} %param.20) | copy-start | bytes 1540
  21.5 121.6 %copy-start.4 = (f32[1,512,128]{2,1,0:T(8,128)S(1)}, f32[1,512,128]{2,1,0:T(8,128)}, u32[]{:S(2)}) copy-start(f32[1,512,128]{2,1,0:T(8,128)} %param.19) | copy-start | bytes 786436
  25.8 122.0 %copy-start.7 = (s32[1,1,128]{2,1,0:T(1,128)S(1)}, s32[1,1,128]{2,1,0:T(1,128)}, u32[]{:S(2)}) copy-start(s32[1,1,128]{2,1,0:T(1,128)} %param.17) | copy-start | bytes 1540
  25.8 122.0 %copy-start.5 = (s32[1,1,1024]{2,1,0:T(1,128)S(1)}, s32[1,1,1024]{2,1,0:T(1,128)}, u32[]{:S(2)}) copy-start(s32[1,1,1024]{2,1,0:T(1,128)} %param.12) | copy-start | bytes 12292
  25.8 198.5 %all-reduce.5.cloned.1.call-start = ((), (), s32[]{:S(2)}) async-start(), calls=%async_computation.1 | async-start | bytes 2097152 | tf_op jit(solution)/shard_map/psum | solution.py:90
  147.9 76.4 %copy-start.3 = (f32[512,512]{1,0:T(8,128)S(1)}, f32[512,512]{1,0:T(8,128)}, u32[]{:S(2)}) copy-start(f32[512,512]{1,0:T(8,128)} %param.21) | copy-start | bytes 3145732
  232.3 2.1 copy-start.2
  252.9 20.6 %copy-start.1 = (bf16[1024,512]{1,0:T(8,128)(2,1)S(1)}, bf16[1024,512]{1,0:T(8,128)(2,1)}, u32[]{:S(2)}) copy-start(bf16[1024,512]{1,0:T(8,128)(2,1)} %gather_fusion.2) | copy-start | bytes 3145732
  254.2 12.1 %collective-permute-start = (bf16[1,256,512]{2,1,0:T(8,128)(2,1)S(1)}, bf16[1,256,512]{2,1,0:T(8,128)(2,1)S(1)}, u32[]{:S(2)}, u32[]{:S(2)}) collective-permute-start(bf16[1,256,512]{2,1,0:T(8,128)(2,1)S(1)} %get-tuple-element.10), channel_id=1, source_target_pairs={{0,8},{8,16},{16,24},{24,32},{32,40},{40,48},{48,56},{56,64},{64,7... | collective-permute-start | bytes 786440 | tf_op jit(solution)/shard_map/ppermute | solution.py:17
  256.2 10.2 %collective-permute-start.1 = (bf16[1,256,512]{2,1,0:T(8,128)(2,1)S(1)}, bf16[1,256,512]{2,1,0:T(8,128)(2,1)S(1)}, u32[]{:S(2)}, u32[]{:S(2)}) collective-permute-start(bf16[1,256,512]{2,1,0:T(8,128)(2,1)S(1)} %get-tuple-element.12), channel_id=1, source_target_pairs={{8,0},{16,8},{24,16},{32,24},{40,32},{48,40},{56,48},{64,56},{72,6... | collective-permute-start | bytes 786440 | tf_op jit(solution)/shard_map/ppermute | solution.py:19
  261.9 7.0 %collective-permute-start.2 = (bf16[1,256,512]{2,1,0:T(8,128)(2,1)S(1)}, bf16[1,256,512]{2,1,0:T(8,128)(2,1)S(1)}, u32[]{:S(2)}, u32[]{:S(2)}) collective-permute-start(bf16[1,256,512]{2,1,0:T(8,128)(2,1)S(1)} %get-tuple-element.11), channel_id=1, source_target_pairs={{0,1},{1,2},{2,3},{3,4},{4,5},{5,6},{6,7},{8,9},{9,10},{10,11},{11... | collective-permute-start | bytes 786440 | tf_op jit(solution)/shard_map/ppermute | solution.py:17
  265.1 8.3 %collective-permute-start.3 = (bf16[1,256,512]{2,1,0:T(8,128)(2,1)S(1)}, bf16[1,256,512]{2,1,0:T(8,128)(2,1)S(1)}, u32[]{:S(2)}, u32[]{:S(2)}) collective-permute-start(bf16[1,256,512]{2,1,0:T(8,128)(2,1)S(1)} %get-tuple-element.13), channel_id=1, source_target_pairs={{1,0},{2,1},{3,2},{4,3},{5,4},{6,5},{7,6},{9,8},{10,9},{11,10},{12... | collective-permute-start | bytes 786440 | tf_op jit(solution)/shard_map/ppermute | solution.py:19
Sparse Core Ops, SparseCore 0:
  25.9 117.1 all-reduce.2
  147.9 76.3 all-reduce.4
where the time goes:
time: 291 us; the launch traced here: 290 us
  waiting for transfers between devices  196 us (67%)
  matrix products  33.3 us (11%)
  between operations  21.9 us (8%)
  local copies, waits for them, and re-layouts  20.7 us (7%)
  starting transfers between devices  12.2 us (4%)
  other arithmetic  5.76 us (2%)
    psum x1, waiting for transfers between devices, shards(): level2_res = lax.psum(contribution, 'sub')  117 us
    psum x1, waiting for transfers between devices, shards(): lax.psum(jnp.dot(selector_three, group_terms, precision=highest), 'grp')  72.2 us
    ppermute x2, starting transfers between devices, extended(): lax.ppermute(head, axis, [((i + 1) % count, i) for i in range(ends)])  7.04 us
  transfers between devices with their start and end apart: 6, of which 4 were waited for; matrix products, arithmetic and copies ran while one was open for 1% of the time, Pallas kernels for 0%

commit v1 on v0

--- a/solution.py
+++ b/solution.py
@@ -85,7 +85,11 @@
     selector_three = (group_map[None, :] == jnp.arange(level3_size)[:, None]).astype(jnp.float32)
     local_part = jnp.dot(local_inverse[0, 0], weighted, preferred_element_type=jnp.float32)
     group_inverse = level2_inverse[0]
-    level2_res = lax.psum(contribution, "sub")
+    level2_res = contribution
+    for hop in (1, 2, 4, 8, 16):
+        level2_res = level2_res + lax.ppermute(
+            level2_res, "sub", [(dev, dev ^ hop) for dev in range(32)]
+        )
     group_terms = lax.dot_general(group_base, level2_res, contract_rows, precision=highest)
     level3_res = lax.psum(jnp.dot(selector_three, group_terms, precision=highest), "grp")
     level2_local = jnp.dot(group_inverse, level2_res, precision=highest)

time: 291 us -> 281 us (0.966)
  waiting for transfers between devices: 196 us -> 174 us
  starting transfers between devices: 12.2 us -> 21.3 us
  local copies, waits for them, and re-layouts: 20.7 us -> 24.5 us
    psum x1 -> x0, waiting for transfers between devices: 117 us -> none  [shards(): level2_res = lax.psum(contribution, 'sub')]
    ppermute x0 -> x5, waiting for transfers between devices: none -> 93.4 us  [shards(): lax.ppermute(level2_res, 'sub', [(dev, dev ^ hop) for dev in range(32)])]
    ppermute x0 -> x5, starting transfers between devices: none -> 9.16 us  [shards(): lax.ppermute(level2_res, 'sub', [(dev, dev ^ hop) for dev in range(32)])]
  transfers between devices with their start and end apart: 6 -> 10, of which waited for: 4 -> 8; matrix products, arithmetic and copies ran while one was open for 1% -> 1% of each run, Pallas kernels for 0% -> 0%
where the time goes in v1:
time: 281 us; the launch traced here: 280 us
  waiting for transfers between devices  174 us (62%)
  matrix products  31.6 us (11%)
  local copies, waits for them, and re-layouts  24.5 us (9%)
  between operations  21.9 us (8%)
  starting transfers between devices  21.3 us (8%)
  other arithmetic  6.59 us (2%)
    ppermute x5, waiting for transfers between devices, shards(): lax.ppermute(level2_res, 'sub', [(dev, dev ^ hop) for dev in range(32)])  93.4 us
    psum x1, waiting for transfers between devices, shards(): lax.psum(jnp.dot(selector_three, group_terms, precision=highest), 'grp')  74 us
    ppermute x5, starting transfers between devices, shards(): lax.ppermute(level2_res, 'sub', [(dev, dev ^ hop) for dev in range(32)])  9.16 us
    ppermute x2, starting transfers between devices, extended(): lax.ppermute(head, axis, [((i + 1) % count, i) for i in range(ends)])  7.04 us
    dot_general x1, matrix products, shards(): level3_sol = jnp.dot(level3_inverse, level3_res, precision=highest)  5.98 us
    dot_general x1, matrix products, shards(): level2_local = jnp.dot(group_inverse, level2_res, precision=highest)  5.9 us
  transfers between devices with their start and end apart: 10, of which 8 were waited for; matrix products, arithmetic and copies ran while one was open for 1% of the time, Pallas kernels for 0%

profile of v1, /device:TPU:8, one launch (start us, length us, event | category | flops | bytes accessed | tf_op | source)
XLA Modules:
  0.0 280.2 jit_solution(16596304576287825161)
XLA Ops:
  7.2 0.0 copy-start
  7.2 0.0 all-reduce.2.cloned.1.call-start
  7.2 1.6 fusion.35
  16.4 5.1 %sort.17 = (s32[1024]{0:T(1024)}, s32[1024]{0:T(1024)S(1)}) sort(s32[1024]{0:T(1024)} %bitcast.80, s32[1024]{0:T(1024)S(1)} %iota.13), dimensions={0}, to_apply=%region_0.0 | sort | flops 10240 | bytes 16384 | tf_op jit(solution)/shard_map/jit(argsort)/sort | solution.py:63
  21.5 0.1 pad_maximum_fusion.1
  21.6 0.1 select_reduce_fusion
  21.6 1.9 fusion.18
  23.6 1.3 fusion.26
  24.9 0.1 collective-permute-start
  25.0 2.6 collective-permute-done
  27.6 0.2 add.107
  27.8 1.6 collective-permute-start.1
  29.4 23.7 %collective-permute-done.1 = f32[512,512]{1,0:T(8,128)S(1)} collective-permute-done((f32[512,512]{1,0:T(8,128)S(1)}, f32[512,512]{1,0:T(8,128)S(1)}, u32[]{:S(2)}, u32[]{:S(2)}) %collective-permute-start.1) | collective-permute-done | bytes 1048608 | tf_op jit(solution)/shard_map/ppermute | solution.py:90
  53.1 0.2 add.108
  53.3 3.1 %collective-permute-start.2 = (f32[512,512]{1,0:T(8,128)S(1)}, f32[512,512]{1,0:T(8,128)S(1)}, u32[]{:S(2)}, u32[]{:S(2)}) collective-permute-start(f32[512,512]{1,0:T(8,128)S(1)} %add.108), channel_id=1, source_target_pairs={{0,32},{8,40},{16,48},{24,56},{32,0},{40,8},{48,16},{56,24},{64,96... | collective-permute-start | bytes 3145736 | tf_op jit(solution)/shard_map/ppermute | solution.py:90
  56.4 22.9 %collective-permute-done.2 = f32[512,512]{1,0:T(8,128)S(1)} collective-permute-done((f32[512,512]{1,0:T(8,128)S(1)}, f32[512,512]{1,0:T(8,128)S(1)}, u32[]{:S(2)}, u32[]{:S(2)}) %collective-permute-start.2) | collective-permute-done | bytes 1048608 | tf_op jit(solution)/shard_map/ppermute | solution.py:90
  79.3 0.2 add.109
  79.5 0.0 copy-start.6
  79.5 0.0 copy-start.4
  79.5 2.3 collective-permute-start.3
  81.8 21.7 %collective-permute-done.3 = f32[512,512]{1,0:T(8,128)S(1)} collective-permute-done((f32[512,512]{1,0:T(8,128)S(1)}, f32[512,512]{1,0:T(8,128)S(1)}, u32[]{:S(2)}, u32[]{:S(2)}) %collective-permute-start.3) | collective-permute-done | bytes 1048608 | tf_op jit(solution)/shard_map/ppermute | solution.py:90
  103.5 0.2 add.110
  103.7 2.1 collective-permute-start.4
  105.8 0.0 copy-done.6
  105.8 0.0 copy-start.5
  105.8 22.4 %collective-permute-done.4 = f32[512,512]{1,0:T(8,128)S(1)} collective-permute-done((f32[512,512]{1,0:T(8,128)S(1)}, f32[512,512]{1,0:T(8,128)S(1)}, u32[]{:S(2)}, u32[]{:S(2)}) %collective-permute-start.4) | collective-permute-done | bytes 1048608 | tf_op jit(solution)/shard_map/ppermute | solution.py:90
  128.3 0.0 copy-start.2
  128.3 1.0 copy-done.2
  129.3 0.0 copy-done.4
  129.3 1.8 fusion.15
  131.1 1.6 fusion.27
  132.7 0.0 all-reduce.2.cloned.1.call-update
  132.7 0.0 copy-done.7
  132.7 0.0 copy-done.5
  132.8 0.0 copy-done
  132.8 4.1 %fusion.3 = f32[512,1024]{1,0:T(8,128)} fusion(bf16[1,1,1024,1024]{3,2,1,0:T(8,128)(2,1)S(1)} %copy-done, bf16[1,1,1024,512]{3,2,1,0:T(8,128)(2,1)} %param.11, f32[1024]{0:T(1024)S(1)} %select_reduce_fusion), kind=kOutput, calls=%fused_computation.8 | convolution fusion | flops 1075314688 | bytes 5246976 | tf_op jit(solution)/shard_map/dot_general | solution.py:86
  136.9 74.0 %all-reduce.2.cloned.1.call-done = f32[512,512]{1,0:T(8,128)} async-done(((f32[512,512]{1,0:T(8,128)}), f32[512,512]{1,0:T(8,128)}) %all-reduce.2.cloned.1.call-update) | async-done | bytes 1048592 | tf_op jit(solution)/shard_map/psum | solution.py:94
  210.8 6.0 %convolution_bitcast_fusion = f32[512,512]{0,1:T(8,128)} fusion(f32[512,512]{1,0:T(8,128)} %all-reduce.2.cloned.1.call-done, f32[512,512]{1,0:T(8,128)} %param.21), kind=kOutput, calls=%fused_computation.15 | convolution fusion | flops 1610612736 | bytes 3145728 | tf_op jit(solution)/shard_map/dot_general | solution.py:96
  216.8 2.5 copy.17
  219.4 2.8 gather_fusion
  222.1 0.0 copy-start.3
  222.1 2.1 fusion.21
  224.2 0.0 copy-done.3
  224.2 5.9 %fusion.12 = f32[512,512]{0,1:T(8,128)} fusion(f32[512,512]{1,0:T(8,128)S(1)} %fusion.21, f32[1,512,512]{2,1,0:T(8,128)} %param.18, f32[512,512]{1,0:T(8,128)S(1)} %add.110, f32[512,512]{1,0:T(8,128)S(1)} %copy-done.3), kind=kOutput, calls=%fused_computation.17 | convolution fusion | flops 1611137024 | bytes 5242880 | tf_op jit(solution)/shard_map/dot_general | solution.py:95
  230.1 1.6 copy.18
  231.7 0.8 gather_fusion.1
  232.4 3.7 %fusion.11 = bf16[1024,512]{0,1:T(8,128)(2,1)} fusion(f32[512,1024]{1,0:T(8,128)} %fusion.3, f32[128,512]{1,0:T(8,128)S(1)} %gather_fusion.1, f32[1024]{0:T(1024)S(1)} %select_reduce_fusion, bf16[1,1,1024,128]{3,2,1,0:T(8,128)(2,1)} %param.16), kind=kOutput, calls=%fused_computation.14 | convolution fusion | flops 806879232 | bytes 3674112 | tf_op jit(solution)/shard_map/dot_general | solution.py:98
  236.2 1.5 copy.19
  237.7 5.1 %gather_fusion.2 = bf16[1024,512]{1,0:T(8,128)(2,1)} fusion(bf16[1024,512]{1,0:T(8,128)(2,1)S(1)} %copy.19, s32[1024]{0:T(1024)S(1)} %broadcast_clamp_fusion), kind=kCustom, calls=%fused_computation.2 | custom fusion | bytes 2101248 | tf_op jit(solution)/shard_map/gather | solution.py:100
  242.8 1.3 slice_bitcast_fusion.3
  244.1 1.9 collective-permute-start.5
  246.1 5.8 %collective-permute-start.6 = (bf16[1,256,512]{2,1,0:T(8,128)(2,1)S(1)}, bf16[1,256,512]{2,1,0:T(8,128)(2,1)S(1)}, u32[]{:S(2)}, u32[]{:S(2)}) collective-permute-start(bf16[1,256,512]{2,1,0:T(8,128)(2,1)S(1)} %get-tuple-element.12), channel_id=1, source_target_pairs={{8,0},{16,8},{24,16},{32,24},{40,32},{48,40},{56,48},{64,56},{72,6... | collective-permute-start | bytes 786440 | tf_op jit(solution)/shard_map/ppermute | solution.py:19
  251.8 3.2 %collective-permute-start.7 = (bf16[1,256,512]{2,1,0:T(8,128)(2,1)S(1)}, bf16[1,256,512]{2,1,0:T(8,128)(2,1)S(1)}, u32[]{:S(2)}, u32[]{:S(2)}) collective-permute-start(bf16[1,256,512]{2,1,0:T(8,128)(2,1)S(1)} %get-tuple-element.11), channel_id=1, source_target_pairs={{0,1},{1,2},{2,3},{3,4},{4,5},{5,6},{6,7},{8,9},{9,10},{10,11},{11... | collective-permute-start | bytes 786440 | tf_op jit(solution)/shard_map/ppermute | solution.py:17
  255.0 1.3 collective-permute-start.8
  256.3 0.0 collective-permute-done.5
  256.3 0.0 collective-permute-done.6
  256.3 2.5 collective-permute-done.7
  258.8 4.4 %collective-permute-done.8 = bf16[1,256,512]{2,1,0:T(8,128)(2,1)S(1)} collective-permute-done((bf16[1,256,512]{2,1,0:T(8,128)(2,1)S(1)}, bf16[1,256,512]{2,1,0:T(8,128)(2,1)S(1)}, u32[]{:S(2)}, u32[]{:S(2)}) %collective-permute-start.8) | collective-permute-done | bytes 262176 | tf_op jit(solution)/shard_map/ppermute | solution.py:19
  263.2 0.1 pad_maximum_fusion
  263.4 0.0 copy-done.1
  263.4 0.4 fusion
  263.8 5.1 %gather_fusion.3 = bf16[1024,512]{1,0:T(8,128)(2,1)} fusion(bf16[1024,512]{1,0:T(8,128)(2,1)S(1)} %fusion, s32[1024]{0:T(1024)S(1)} %get-tuple-element.14), kind=kCustom, calls=%fused_computation.3 | custom fusion | bytes 2101248 | tf_op jit(solution)/shard_map/gather | solution.py:105
  268.8 3.2 %fusion.8 = bf16[1,1,1024,512]{2,3,1,0:T(8,128)(2,1)S(1)} fusion(bf16[1024,512]{1,0:T(8,128)(2,1)} %gather_fusion.3, bf16[1,1,1024,1024]{3,2,1,0:T(8,128)(2,1)} %param.14), kind=kOutput, calls=%fused_computation.13 | convolution fusion | flops 1074266112 | bytes 4194304 | tf_op jit(solution)/shard_map/dot_general | solution.py:106
  272.1 1.3 copy.20
  (10 shorter events, 0.0 us)
Async XLA Ops:
  7.2 125.6 %copy-start = (bf16[1,1,1024,1024]{3,2,1,0:T(8,128)(2,1)S(1)}, bf16[1,1,1024,1024]{3,2,1,0:T(8,128)(2,1)}, u32[]{:S(2)}) copy-start(bf16[1,1,1024,1024]{3,2,1,0:T(8,128)(2,1)} %param.15) | copy-start | bytes 6291460
  7.2 203.7 %all-reduce.2.cloned.1.call-start = ((), (), s32[]{:S(2)}) async-start(), calls=%async_computation | async-start | bytes 2097152 | tf_op jit(solution)/shard_map/psum | solution.py:94
  24.9 2.7 collective-permute-start
  27.8 25.3 %collective-permute-start.1 = (f32[512,512]{1,0:T(8,128)S(1)}, f32[512,512]{1,0:T(8,128)S(1)}, u32[]{:S(2)}, u32[]{:S(2)}) collective-permute-start(f32[512,512]{1,0:T(8,128)S(1)} %add.107), channel_id=1, source_target_pairs={{0,16},{8,24},{16,0},{24,8},{32,48},{40,56},{48,32},{56,40},{64,80... | collective-permute-start | bytes 3145736 | tf_op jit(solution)/shard_map/ppermute | solution.py:90
  53.3 26.0 %collective-permute-start.2 = (f32[512,512]{1,0:T(8,128)S(1)}, f32[512,512]{1,0:T(8,128)S(1)}, u32[]{:S(2)}, u32[]{:S(2)}) collective-permute-start(f32[512,512]{1,0:T(8,128)S(1)} %add.108), channel_id=1, source_target_pairs={{0,32},{8,40},{16,48},{24,56},{32,0},{40,8},{48,16},{56,24},{64,96... | collective-permute-start | bytes 3145736 | tf_op jit(solution)/shard_map/ppermute | solution.py:90
  79.5 26.3 %copy-start.6 = (s32[1,128]{1,0:T(1,128)S(1)}, s32[1,128]{1,0:T(1,128)}, u32[]{:S(2)}) copy-start(s32[1,128]{1,0:T(1,128)} %param.20) | copy-start | bytes 1540
  79.5 49.8 %copy-start.4 = (f32[1,512,128]{2,1,0:T(8,128)S(1)}, f32[1,512,128]{2,1,0:T(8,128)}, u32[]{:S(2)}) copy-start(f32[1,512,128]{2,1,0:T(8,128)} %param.19) | copy-start | bytes 786436
  79.5 24.0 %collective-permute-start.3 = (f32[512,512]{1,0:T(8,128)S(1)}, f32[512,512]{1,0:T(8,128)S(1)}, u32[]{:S(2)}, u32[]{:S(2)}) collective-permute-start(f32[512,512]{1,0:T(8,128)S(1)} %add.109), channel_id=1, source_target_pairs={{0,64},{8,72},{16,80},{24,88},{32,96},{40,104},{48,112},{56,120},{... | collective-permute-start | bytes 3145736 | tf_op jit(solution)/shard_map/ppermute | solution.py:90
  103.7 24.6 %collective-permute-start.4 = (f32[512,512]{1,0:T(8,128)S(1)}, f32[512,512]{1,0:T(8,128)S(1)}, u32[]{:S(2)}, u32[]{:S(2)}) collective-permute-start(f32[512,512]{1,0:T(8,128)S(1)} %add.110), channel_id=1, source_target_pairs={{0,128},{8,136},{16,144},{24,152},{32,160},{40,168},{48,176},{56,1... | collective-permute-start | bytes 3145736 | tf_op jit(solution)/shard_map/ppermute | solution.py:90
  105.8 26.8 %copy-start.7 = (s32[1,1,128]{2,1,0:T(1,128)S(1)}, s32[1,1,128]{2,1,0:T(1,128)}, u32[]{:S(2)}) copy-start(s32[1,1,128]{2,1,0:T(1,128)} %param.17) | copy-start | bytes 1540
  105.8 26.9 %copy-start.5 = (s32[1,1,1024]{2,1,0:T(1,128)S(1)}, s32[1,1,1024]{2,1,0:T(1,128)}, u32[]{:S(2)}) copy-start(s32[1,1,1024]{2,1,0:T(1,128)} %param.12) | copy-start | bytes 12292
  128.3 1.0 copy-start.2
  222.1 2.1 copy-start.3
  242.8 20.6 %copy-start.1 = (bf16[1024,512]{1,0:T(8,128)(2,1)S(1)}, bf16[1024,512]{1,0:T(8,128)(2,1)}, u32[]{:S(2)}) copy-start(bf16[1024,512]{1,0:T(8,128)(2,1)} %gather_fusion.2) | copy-start | bytes 3145732
  244.1 12.2 %collective-permute-start.5 = (bf16[1,256,512]{2,1,0:T(8,128)(2,1)S(1)}, bf16[1,256,512]{2,1,0:T(8,128)(2,1)S(1)}, u32[]{:S(2)}, u32[]{:S(2)}) collective-permute-start(bf16[1,256,512]{2,1,0:T(8,128)(2,1)S(1)} %get-tuple-element.10), channel_id=1, source_target_pairs={{0,8},{8,16},{16,24},{24,32},{32,40},{40,48},{48,56},{56,64},{64,7... | collective-permute-start | bytes 786440 | tf_op jit(solution)/shard_map/ppermute | solution.py:17
  246.1 10.2 %collective-permute-start.6 = (bf16[1,256,512]{2,1,0:T(8,128)(2,1)S(1)}, bf16[1,256,512]{2,1,0:T(8,128)(2,1)S(1)}, u32[]{:S(2)}, u32[]{:S(2)}) collective-permute-start(bf16[1,256,512]{2,1,0:T(8,128)(2,1)S(1)} %get-tuple-element.12), channel_id=1, source_target_pairs={{8,0},{16,8},{24,16},{32,24},{40,32},{48,40},{56,48},{64,56},{72,6... | collective-permute-start | bytes 786440 | tf_op jit(solution)/shard_map/ppermute | solution.py:19
  251.8 7.0 %collective-permute-start.7 = (bf16[1,256,512]{2,1,0:T(8,128)(2,1)S(1)}, bf16[1,256,512]{2,1,0:T(8,128)(2,1)S(1)}, u32[]{:S(2)}, u32[]{:S(2)}) collective-permute-start(bf16[1,256,512]{2,1,0:T(8,128)(2,1)S(1)} %get-tuple-element.11), channel_id=1, source_target_pairs={{0,1},{1,2},{2,3},{3,4},{4,5},{5,6},{6,7},{8,9},{9,10},{10,11},{11... | collective-permute-start | bytes 786440 | tf_op jit(solution)/shard_map/ppermute | solution.py:17
  255.0 8.3 %collective-permute-start.8 = (bf16[1,256,512]{2,1,0:T(8,128)(2,1)S(1)}, bf16[1,256,512]{2,1,0:T(8,128)(2,1)S(1)}, u32[]{:S(2)}, u32[]{:S(2)}) collective-permute-start(bf16[1,256,512]{2,1,0:T(8,128)(2,1)S(1)} %get-tuple-element.13), channel_id=1, source_target_pairs={{1,0},{2,1},{3,2},{4,3},{5,4},{6,5},{7,6},{9,8},{10,9},{11,10},{12... | collective-permute-start | bytes 786440 | tf_op jit(solution)/shard_map/ppermute | solution.py:19
Sparse Core Ops, SparseCore 0:
  132.8 77.9 all-reduce.1
